TPU v7x, 256 devices: a whole 4x4x8 slice. The times are simulated.
256 devices in a mesh: gx: 8 (over y, core), gy: 32 (over x, z).
Axes of the slice: x: 4, y: 4, z: 8, core: 2. Of those that a mesh axis runs over, the one named last changes fastest.
Arguments:
- field: bfloat16 [1024, 256, 512], P('gx', 'gy'), may hold values from -6 to 6
- conv_weight: bfloat16 [27, 32, 32], replicated, may hold values from -0.21875 to 0.21875
- conv_bias: float32 [32], replicated, may hold values from -3 to 3
- spectral_weight: bfloat16 [32, 2, 32, 32], replicated, may hold values from -2 to 2
Outputs:
- layer_out: bfloat16 [1024, 256, 512], P('gx', 'gy')
All inputs are finite; a program needn't handle non-finite values.
Results may differ from a plain program's by a relative error of at most 0.0049.
Values may be sent and summed in bfloat16 or wider, within the bound.
A program may use at most 128 MiB of HBM per device.

v0:
```python
import functools
import math

import jax
import jax.numpy as jnp
import numpy as np
from jax import lax
from jax.experimental import pallas as pl
from jax.experimental.pallas import tpu as pltpu
from jax.sharding import PartitionSpec as P

MESH = pl.DeviceIdType.MESH
CHUNKS = 2
SPLIT_ROW = 96
FIRST_BANDS = 0
SHARE = ((SPLIT_ROW, 128 - SPLIT_ROW), (0, SPLIT_ROW))
FAR_FIRST = (1, 0, 2)
F32 = jnp.float32
BF16 = jnp.bfloat16


def dot(a, b):
    return jnp.dot(a, b, preferred_element_type=F32)


def expanded_tables(length, modes, groups, rows_y):
    turns = (np.arange(modes)[:, None] * np.arange(length)[None, :]) % length
    angles = turns.astype(np.float32) * np.float32(2.0 * math.pi / length)
    pairs = np.stack([np.cos(angles), -np.sin(angles)], axis=1) * np.float32(1.0 / math.sqrt(length))
    doubling = np.where(np.arange(modes) == 0, 1.0, 2.0).astype(np.float32)
    forward = pairs.reshape(2 * modes, groups, length // groups).transpose(1, 0, 2)
    inverse = (pairs * doubling[:, None, None]).reshape(2 * modes, groups, length // groups).transpose(1, 2, 0)
    forward = np.repeat(forward, rows_y, axis=2)
    inverse = np.kron(inverse, np.eye(rows_y, dtype=np.float32))
    return jnp.asarray(forward, BF16), jnp.asarray(inverse, BF16)


def spread(table_ref, out_ref):
    rows, lanes = table_ref.shape

    def body(i, carry):
        part = table_ref[pl.ds(pl.multiple_of(i * 16, 16), 16), :].astype(F32)
        wide = jnp.broadcast_to(part[:, None, :], (16, 8, lanes))
        keep = lax.broadcasted_iota(jnp.int32, (16, 8, lanes), 1) == (
            lax.broadcasted_iota(jnp.int32, (16, 8, lanes), 2) & 7
        )
        out_ref[pl.ds(pl.multiple_of(i * 128, 128), 128), :] = (
            jnp.where(keep, wide, 0.0).reshape(128, lanes).astype(BF16)
        )
        return carry

    lax.fori_loop(0, rows // 16, body, 0)


def layer_kernel(
    field, convw, bias, specw, ftab, itab, out,
    fs, fexp, cw, sw, bv, amat, gmat, wrep, tmat, cmat, rmat, conv,
    part, cbuf, cland, rland, mixed, ybuf, yland, xland, cornl,
    load_sem, bar_send, c_send, c_recv, r_send, r_recv, a_send, a_recv, f_send, f_recv,
    x_send, x_recv, y_send, y_recv, k_send, k_recv, ready,
):
    nch, _, lc = mixed.shape
    tiles = lc // 128
    g = lax.axis_index("gx")
    h = lax.axis_index("gy")
    ng = lax.axis_size("gx")
    nh = lax.axis_size("gy")
    ny = ng // 2
    yc, core = g // 2, g % 2
    sib = (2 * yc + (1 - core), h)

    def ychip(j):
        return (2 * lax.rem(yc + j, ny) + core, h)

    left, right = lax.rem(g + ng - 1, ng), lax.rem(g + 1, ng)
    prev, nxt = lax.rem(h + nh - 1, nh), lax.rem(h + 1, nh)
    outer = lax.rem(g + ng + 2 * core - 1, ng)

    def remote(src, dst, s, r, dev):
        return pltpu.make_async_remote_copy(
            src_ref=src, dst_ref=dst, send_sem=s, recv_sem=r, device_id=dev, device_id_type=MESH
        )

    load_f = pltpu.make_async_copy(ftab.at[g], fexp, load_sem.at[0])
    load_x = pltpu.make_async_copy(field, fs.at[1, pl.ds(1, 128)], load_sem.at[1])
    load_i = pltpu.make_async_copy(itab.at[g], gmat, load_sem.at[2])
    load_w = pltpu.make_async_copy(convw, cw, load_sem.at[3])
    load_s = pltpu.make_async_copy(specw.at[pl.ds(8 * yc, 8)], sw, load_sem.at[4])
    load_b = pltpu.make_async_copy(bias, bv, load_sem.at[5])
    for load in (load_f, load_x, load_w, load_s, load_b, load_i):
        load.start()

    barrier = pltpu.get_barrier_semaphore()
    chips = [ychip(j) for j in range(1, ny)]
    for dev in [sib, (outer, h)] + chips:
        pl.semaphore_signal(barrier, inc=1, device_id=dev, device_id_type=MESH)
    first_up = lax.rem(h + 1, 8) != 0
    first_down = lax.rem(h, 8) == 0
    has_up, has_down = h < nh - 1, h > 0
    pairs = [
        (has_down, first_down, (g, prev), 1),
        (has_up, first_up, (g, nxt), 0),
    ]
    waits = jnp.int32(2 + len(chips))
    for there, first, dev, _ in pairs:

        @pl.when(there & first)
        def _(dev=dev):
            pl.semaphore_signal(barrier, inc=1, device_id=dev, device_id_type=MESH)

        waits = waits + jnp.where(there & ~first, 1, 0)

    load_f.wait()
    spread(fexp, amat)
    load_w.wait()
    rep8 = jnp.where(
        (lax.broadcasted_iota(jnp.int32, (32, 256), 1) & 31) == lax.broadcasted_iota(jnp.int32, (32, 256), 0), 1.0, 0.0
    ).astype(BF16)
    wrep[...] = dot(cw[...].reshape(864, 32), rep8)
    zlane8 = lax.broadcasted_iota(jnp.int32, (32, 256), 1) // 32
    cmat[...] = jnp.zeros_like(cmat)

    def band(t, carry):
        dyi, dxi = t // 3, t % 3
        base = pl.multiple_of((dxi * 3 + dyi) * 96, 32)
        w = [wrep[pl.ds(pl.multiple_of(base + 32 * k, 32), 32), :] for k in range(3)]
        for z in range(8):
            block = jnp.where(zlane8 == z + 1, w[0], 0.0)
            block = jnp.where(zlane8 == z, w[1], block)
            block = jnp.where(zlane8 == z - 1, w[2], block)
            tmat[pl.ds(pl.multiple_of(t * 256 + z * 32, 32), 32), :] = block.astype(BF16)
        cmat[pl.ds(pl.multiple_of(t * 256 + 96, 32), 32), :] = jnp.where(zlane8 == 4, w[0], 0.0).astype(BF16)
        cmat[pl.ds(pl.multiple_of(t * 256 + 128, 32), 32), :] = jnp.where(zlane8 == 3, w[2], 0.0).astype(BF16)
        return carry

    lax.fori_loop(0, FIRST_BANDS, band, 0)
    load_x.wait()
    def rows_of(chip, c):
        return pl.ds(pl.multiple_of(chip * 128 + SHARE[c][0], 16), SHARE[c][1])

    def aims(j, c):
        return rows_of(lax.rem(yc + j, ny), c)

    order = [(ch, j) for ch in range(nch) for j in (2, 1, 3)] + [(ch, 0) for ch in range(nch)]

    def c_copy(ch, j, owner):
        return remote(cbuf.at[ch, aims(j, owner)], cland.at[ch, aims(j, owner)], c_send.at[ch, j], c_recv.at[ch, j], sib)

    def r_copy(ch, j, c):
        return remote(
            cbuf.at[ch, aims(j, c)], rland.at[ch, j - 1, pl.ds(*SHARE[c])],
            r_send.at[ch, j - 1], r_recv.at[ch, j - 1], ychip(j),
        )

    def a_copy(ch, j, c):
        block = mixed.at[ch, aims(0, c)]
        return remote(block, block, a_send.at[ch, j - 1], a_recv.at[ch, j - 1], ychip(j))

    def f_copy(ch, j, c):
        block = mixed.at[ch, aims(ny - j, c)]
        return remote(block, block, f_send.at[ch, j], f_recv.at[ch, j], sib)

    value = dot(amat[...], fs[1, 1:129].reshape(1024, 512))
    for ch in range(nch):
        part[ch] = value[:, ch * lc : (ch + 1) * lc]
    pl.semaphore_wait(barrier, waits)

    def send_sums(c):
        for ch, j in order:
            cbuf[ch, aims(j, 1 - c), :] = part[ch, aims(j, 1 - c), :].astype(BF16)
            c_copy(ch, j, 1 - c).start()

    for c in range(2):
        pl.when(core == c)(functools.partial(send_sums, c))

    for there, first, dev, lands in pairs:

        @pl.when(there & ~first)
        def _(dev=dev, lands=lands):
            pl.semaphore_signal(ready.at[lands], inc=1, device_id=dev, device_id_type=MESH)

    x_copies = [
        remote(fs.at[1, pl.ds(127, 2)], xland.at[0], x_send.at[0], x_recv.at[0], (right, h)),
        remote(fs.at[1, pl.ds(1, 2)], xland.at[1], x_send.at[1], x_recv.at[1], (left, h)),
    ]
    for copy in x_copies:
        copy.start()
    def pass_sums(c):
        for ch, j in order:
            c_copy(ch, j, c).wait_recv()
            if j > 0:
                total = part[ch, aims(j, c), :] + cland[ch, aims(j, c), :].astype(F32)
                cbuf[ch, aims(j, c), :] = total.astype(BF16)
                r_copy(ch, j, c).start()

    for c in range(2):
        pl.when(core == c)(functools.partial(pass_sums, c))

    load_s.wait()

    def modes_of(c):
        return range(SHARE[c][0] // 16, (SHARE[c][0] + SHARE[c][1]) // 16)

    def mixing_weights(c):
        rep4 = jnp.where(
            (lax.broadcasted_iota(jnp.int32, (32, 128), 1) & 31) == lax.broadcasted_iota(jnp.int32, (32, 128), 0), 1.0, 0.0
        ).astype(BF16)
        sv = dot(sw[...].reshape(512, 32), rep4)
        zlane = lax.broadcasted_iota(jnp.int32, (32, 128), 1) // 32
        for m in modes_of(c):
            wr = sv[m * 64 : m * 64 + 32]
            wi = sv[m * 64 + 32 : m * 64 + 64]
            for r in range(2):
                for z in range(4):
                    first = jnp.where(zlane == z, wr if r == 0 else -wi, 0.0)
                    second = jnp.where(zlane == z, wi if r == 0 else wr, 0.0)
                    rmat[m, r * 128 + z * 32 : r * 128 + z * 32 + 32, :] = jnp.concatenate([first, second], axis=1).astype(BF16)

    for c in range(2):
        pl.when(core == c)(functools.partial(mixing_weights, c))

    row = lax.broadcasted_iota(jnp.int32, (64, 256), 0)
    col = lax.broadcasted_iota(jnp.int32, (64, 256), 1)
    pick = jnp.where(col == (row & 31) * 8 + jnp.where(row < 32, 7, 0), 1.0, 0.0).astype(BF16)
    for b in range(4):
        cells = fs[1, 1 + 32 * b : 33 + 32 * b].reshape(256, 512)
        picked = dot(pick, cells).astype(BF16)
        ybuf[0, 32 * b : 32 * b + 32, :] = picked[:32]
        ybuf[1, 32 * b : 32 * b + 32, :] = picked[32:]
    y_copies = [
        remote(ybuf.at[1], yland.at[1], y_send.at[1], y_recv.at[1], (g, prev)),
        remote(ybuf.at[0], yland.at[0], y_send.at[0], y_recv.at[0], (g, nxt)),
    ]
    k_copies = [
        remote(xland, cornl.at[1], k_send.at[1], k_recv.at[1], (g, prev)),
        remote(xland, cornl.at[0], k_send.at[0], k_recv.at[0], (g, nxt)),
    ]
    for (there, first, _, _), copy in zip(pairs, y_copies):
        pl.when(there & ~first)(copy.start)

    lax.fori_loop(FIRST_BANDS, 9, band, 0)

    def shift(first, count):
        cells = fs[1, pl.ds(first, count)].astype(F32)
        sub = lax.broadcasted_iota(jnp.int32, cells.shape, 1)
        fs[0, pl.ds(first, count)] = jnp.where(sub == 0, 0.0, pltpu.roll(cells, 1, 1)).astype(BF16)
        fs[2, pl.ds(first, count)] = jnp.where(sub == 7, 0.0, pltpu.roll(cells, 7, 1)).astype(BF16)

    def shift_block(b, carry):
        shift(1 + b * 32, 32)
        return carry

    lax.fori_loop(0, 4, shift_block, 0)
    for copy in x_copies:
        copy.wait()
    has_left = jnp.where(g > 0, 1.0, 0.0)
    has_right = jnp.where(g < ng - 1, 1.0, 0.0)
    for (there, first, _, _), copy in zip(pairs, k_copies):
        pl.when(there & ~first)(copy.start)

    def greet_later(far):
        k = 0 if far else 1
        there, first, _, _ = pairs[k]

        @pl.when(there & first)
        def _():
            pl.semaphore_wait(ready.at[k], 1)
            y_copies[k].start()
            k_copies[k].start()

    greet_later(False)
    fs[1, 0:1] = (xland[0, 1:2].astype(F32) * has_left).astype(BF16)
    fs[1, 129:130] = (xland[1, 0:1].astype(F32) * has_right).astype(BF16)
    shift(0, 1)
    shift(129, 1)

    load_b.wait()
    bias_row = jnp.concatenate([bv[...]] * 16, axis=1)

    def windows(taps, first, count):
        low = jnp.concatenate([t[:, :256] for t in taps], axis=1)
        high = jnp.concatenate([t[:, 256:] for t in taps], axis=1)
        mid = jnp.concatenate([t[:, 128:384] for t in taps], axis=1)
        rows = low.shape[0]
        main = dot(jnp.concatenate([low, high], axis=0), tmat[first : first + count, :])
        cross = dot(mid, cmat[first : first + count, :])
        return jnp.concatenate(
            [
                main[:rows, :128], main[:rows, 128:] + cross[:, :128],
                main[rows:, :128] + cross[:, 128:], main[rows:, 128:],
            ],
            axis=1,
        )

    def conv_block(b, carry):
        taps = [fs[dy, pl.ds(b * 32 + dx, 32)].reshape(256, 512) for dy in range(3) for dx in range(3)]
        value = windows(taps, 0, 2304) + bias_row
        for t in range(4):
            conv[t, pl.ds(pl.multiple_of(b * 256, 256), 256), :] = value[:, 128 * t : 128 * t + 128]
        return carry

    lax.fori_loop(0, 2, conv_block, 0, unroll=True)

    def mix_modes(c):
        first, count = SHARE[c]
        for ch in range(nch):
            coef = part[ch, aims(0, c), :] + cland[ch, aims(0, c), :].astype(F32)
            for j in range(1, ny):
                r_copy(ch, j, c).wait_recv()
                coef = coef + rland[ch, j - 1, first : first + count, :].astype(F32)
            pieces = []
            for m in modes_of(c):
                at = m * 16 - first
                rows = jnp.concatenate(
                    [
                        jnp.concatenate(
                            [coef[at + 8 * r : at + 8 * r + 8, 128 * t : 128 * t + 128] for r in range(2)], axis=1
                        )
                        for t in range(tiles)
                    ],
                    axis=0,
                ).astype(BF16)
                mix = dot(rows, rmat[m])
                for r in range(2):
                    pieces.append(
                        jnp.concatenate([mix[8 * t : 8 * t + 8, 128 * r : 128 * r + 128] for t in range(tiles)], axis=1)
                    )
            mixed[ch, aims(0, c), :] = jnp.concatenate(pieces, axis=0).astype(BF16)
            for k in FAR_FIRST:
                a_copy(ch, k + 1, c).start()
            f_copy(ch, 0, c).start()

    for c in range(2):
        pl.when(core == c)(functools.partial(mix_modes, c))

    greet_later(True)

    lax.fori_loop(2, 4, conv_block, 0, unroll=True)

    row = lax.broadcasted_iota(jnp.int32, (256, 160), 0)
    col = lax.broadcasted_iota(jnp.int32, (256, 160), 1)
    x = row & 127
    def halo(side, here):
        @pl.when(pairs[side][0] & here)
        def _():
            y_copies[1 - side].wait_recv()
            k_copies[1 - side].wait_recv()
            yrow = 7 if side == 0 else 0
            inside = jnp.where(row < 128, x - 1, x + 1)
            picks = jnp.where((col == inside) & (col < 128), 1.0, 0.0)
            picks = jnp.where((row == 0) & (col == 128 + 8 + yrow), has_left, picks)
            picks = jnp.where((row == 255) & (col == 128 + 16 + yrow), has_right, picks)
            mid_rows = yland[side]
            source = jnp.concatenate([mid_rows, cornl[side].reshape(32, 512)], axis=0)
            moved = dot(picks.astype(BF16), source).astype(BF16)
            value = windows([moved[:128], mid_rows, moved[128:]], 1536 * side, 768)
            edge = pl.ds(0 if side == 0 else 7, 128, stride=8)
            for t in range(4):
                conv[t, edge, :] = conv[t, edge, :] + value[:, 128 * t : 128 * t + 128]

    far_first = lax.rem(h, 8) == 0
    halo(1, h >= 0)
    halo(0, ~far_first)

    def pass_mixed(c):
        for ch in range(nch):
            for j in (1, 3, 2):
                a_copy(ch, j, c).wait_recv()
                f_copy(ch, j, c).start()

    for c in range(2):
        pl.when(core == c)(functools.partial(pass_mixed, c))

    halo(0, far_first)

    load_i.wait()
    for ch in range(nch):

        def wait_mixed(c, ch=ch):
            for j in range(ny):
                f_copy(ch, j, 1 - c).wait_recv()

        for c in range(2):
            pl.when(core == c)(functools.partial(wait_mixed, c))

        def finish(b, carry):
            rows = pl.ds(pl.multiple_of(b * 256, 256), 256)
            lanes = slice(ch * lc, (ch + 1) * lc)
            base = jnp.concatenate([conv[ch * tiles + t, rows, :] for t in range(tiles)], axis=1)
            value = dot(gmat[rows, :], mixed[ch]) + base
            value = 0.5 * value * (1.0 + lax.erf(value * (0.5**0.5)))
            out[pl.ds(b * 32, 32), :, lanes] = value.reshape(32, 8, lc).astype(BF16)
            return carry

        lax.fori_loop(0, 4, finish, 0, unroll=True)

    def wait_sends(c):
        for ch in range(nch):
            for j in range(ny):
                c_copy(ch, j, 1 - c).wait_send()
                f_copy(ch, j, c).wait_send()
            for j in range(1, ny):
                r_copy(ch, j, c).wait_send()
                a_copy(ch, j, c).wait_send()

    for c in range(2):
        pl.when(core == c)(functools.partial(wait_sends, c))

    for (there, _, _, _), y_copy, k_copy in zip(pairs, y_copies, k_copies):

        @pl.when(there)
        def _(y_copy=y_copy, k_copy=k_copy):
            y_copy.wait_send()
            k_copy.wait_send()


def shards(field, conv_weight, conv_bias, spectral_weight):
    cells_x, cells_y, width = field.shape
    groups = lax.axis_size("gx")
    modes = spectral_weight.shape[0]
    ny = groups // 2
    lc = width // CHUNKS
    ftab, itab = expanded_tables(cells_x * groups, modes, groups, cells_y)
    dma = pltpu.SemaphoreType.DMA
    vmem = pltpu.VMEM
    scratch = [
        vmem((3, cells_x + 2, cells_y, width), BF16),
        vmem((64, 1024), BF16),
        vmem((27, 32, 32), BF16),
        vmem((8, 2, 32, 32), BF16),
        vmem((1, 32), F32),
        vmem((512, 1024), BF16),
        vmem((1024, 512), BF16),
        vmem((864, 256), F32),
        vmem((2304, 256), BF16),
        vmem((2304, 256), BF16),
        vmem((8, 256, 256), BF16),
        vmem((4, 1024, 128), F32),
        vmem((CHUNKS, 512, lc), F32),
        vmem((CHUNKS, 512, lc), BF16),
        vmem((CHUNKS, 512, lc), BF16),
        vmem((CHUNKS, ny - 1, 128, lc), BF16),
        vmem((CHUNKS, 512, lc), BF16),
        vmem((2, 128, 512), BF16),
        vmem((2, 128, 512), BF16),
        vmem((2, 2, 8, 512), BF16),
        vmem((2, 2, 2, 8, 512), BF16),
        dma((6,)), dma((1,)),
        dma((CHUNKS, ny)), dma((CHUNKS, ny)),
        dma((CHUNKS, ny - 1)), dma((CHUNKS, ny - 1)),
        dma((CHUNKS, ny - 1)), dma((CHUNKS, ny - 1)),
        dma((CHUNKS, ny)), dma((CHUNKS, ny)),
        dma((2,)), dma((2,)), dma((2,)), dma((2,)), dma((2,)), dma((2,)),
        pltpu.SemaphoreType.REGULAR((2,)),
    ]
    operands = (field, conv_weight, conv_bias.reshape(1, -1), spectral_weight, ftab, itab)
    in_hbm = pl.BlockSpec(memory_space=pltpu.HBM)
    return pl.pallas_call(
        layer_kernel,
        out_shape=jax.ShapeDtypeStruct(field.shape, BF16),
        in_specs=[in_hbm] * 6,
        out_specs=pl.BlockSpec(memory_space=pltpu.VMEM),
        scratch_shapes=scratch,
        compiler_params=pltpu.CompilerParams(
            collective_id=0, has_side_effects=True, vmem_limit_bytes=40 * 1024 * 1024
        ),
        name="layer",
    )(*(pltpu.with_memory_space_constraint(a, pltpu.HBM) for a in operands))


def solution(mesh):
    placed = (P("gx", "gy", None), P(), P(), P())
    return jax.shard_map(
        shards, mesh=mesh, in_specs=placed, out_specs=P("gx", "gy", None), check_vma=False
    )
```

profile of v0, /device:TPU:7, one launch (start us, length us, event | category | flops | bytes accessed | tf_op | source)
XLA Modules:
  0.0 18.5 jit_solution(8451904046578902405)
XLA Ops:
  0.0 17.5 %layer.1 = bf16[128,8,512]{2,1,0:T(8,128)(2,1)S(1)} custom-call(bf16[128,8,512]{2,1,0:T(8,128)(2,1)} %field.1, bf16[27,32,32]{2,1,0:T(8,128)(2,1)} %convw.1, f32[1,32]{1,0:T(1,128)} %bitcast.1, bf16[32,2,32,32]{3,2,1,0:T(8,128)(2,1)} %specw.1, bf16[8,64,1024]{2,1,0:T(8,128)(2,1)} %constant.4.clone.ftab, bf16[8,1024,512]{2,1,0:T(8,128)(2,1)} %constant.5.clone.itab), custom_call_target="tpu_custom_call" | custom-call | tf_op jit(solution)/shard_map/layer/pallas_call | solution.py:458
  17.5 1.0 %copy.8 = bf16[128,8,512]{2,1,0:T(8,128)(2,1)} copy(bf16[128,8,512]{2,1,0:T(8,128)(2,1)S(1)} %layer.1) | data formatting | bytes 2097152
where the time goes:
time: 18.5 us
  Pallas kernels  17.5 us (95%)
  local copies, waits for them, and re-layouts  0.97 us (5%)
    pallas_call x1, Pallas kernels, shards(): pl.pallas_call(layer_kernel, out_shape=jax.ShapeDtypeStruct(field.shape,...  17.5 us
    unnamed x1, local copies, waits for them, and re-layouts  0.97 us

commit v1 on v0

--- a/solution.py
+++ b/solution.py
@@ -333,9 +333,8 @@
     for c in range(2):
         pl.when(core == c)(functools.partial(mix_modes, c))
 
+    lax.fori_loop(2, 4, conv_block, 0, unroll=True)
     greet_later(True)
-
-    lax.fori_loop(2, 4, conv_block, 0, unroll=True)
 
     row = lax.broadcasted_iota(jnp.int32, (256, 160), 0)
     col = lax.broadcasted_iota(jnp.int32, (256, 160), 1)

time: 18.5 us -> 19.2 us (1.038)
  the two profiles are of different devices: /device:TPU:7 before, /device:TPU:227 now
where the time goes in v1:
time: 19.2 us; the launch traced here: 19.1 us
  Pallas kernels  18.2 us (95%)
  local copies, waits for them, and re-layouts  0.97 us (5%)
    pallas_call x1, Pallas kernels, shards(): pl.pallas_call(layer_kernel, out_shape=jax.ShapeDtypeStruct(field.shape,...  18.2 us
    unnamed x1, local copies, waits for them, and re-layouts  0.97 us

profile of v1, /device:TPU:227, one launch (start us, length us, event | category | flops | bytes accessed | tf_op | source)
XLA Modules:
  0.0 19.1 jit_solution(13483992425652482777)
XLA Ops:
  0.0 18.2 %layer.1 = bf16[128,8,512]{2,1,0:T(8,128)(2,1)S(1)} custom-call(bf16[128,8,512]{2,1,0:T(8,128)(2,1)} %field.1, bf16[27,32,32]{2,1,0:T(8,128)(2,1)} %convw.1, f32[1,32]{1,0:T(1,128)} %bitcast.1, bf16[32,2,32,32]{3,2,1,0:T(8,128)(2,1)} %specw.1, bf16[8,64,1024]{2,1,0:T(8,128)(2,1)} %constant.4.clone.ftab, bf16[8,1024,512]{2,1,0:T(8,128)(2,1)} %constant.5.clone.itab), custom_call_target="tpu_custom_call" | custom-call | tf_op jit(solution)/shard_map/layer/pallas_call | solution.py:457
  18.2 1.0 %copy.8 = bf16[128,8,512]{2,1,0:T(8,128)(2,1)} copy(bf16[128,8,512]{2,1,0:T(8,128)(2,1)S(1)} %layer.1) | data formatting | bytes 2097152

commit v2 on v1

--- a/solution.py
+++ b/solution.py
@@ -170,14 +170,17 @@
             cbuf[ch, aims(j, 1 - c), :] = part[ch, aims(j, 1 - c), :].astype(BF16)
             c_copy(ch, j, 1 - c).start()
 
+    def answer(k):
+        there, first, dev, lands = pairs[k]
+
+        @pl.when(there & ~first)
+        def _():
+            pl.semaphore_signal(ready.at[lands], inc=1, device_id=dev, device_id_type=MESH)
+
+    answer(1)
     for c in range(2):
         pl.when(core == c)(functools.partial(send_sums, c))
-
-    for there, first, dev, lands in pairs:
-
-        @pl.when(there & ~first)
-        def _(dev=dev, lands=lands):
-            pl.semaphore_signal(ready.at[lands], inc=1, device_id=dev, device_id_type=MESH)
+    answer(0)
 
     x_copies = [
         remote(fs.at[1, pl.ds(127, 2)], xland.at[0], x_send.at[0], x_recv.at[0], (right, h)),
@@ -195,29 +198,6 @@
 
     for c in range(2):
         pl.when(core == c)(functools.partial(pass_sums, c))
-
-    load_s.wait()
-
-    def modes_of(c):
-        return range(SHARE[c][0] // 16, (SHARE[c][0] + SHARE[c][1]) // 16)
-
-    def mixing_weights(c):
-        rep4 = jnp.where(
-            (lax.broadcasted_iota(jnp.int32, (32, 128), 1) & 31) == lax.broadcasted_iota(jnp.int32, (32, 128), 0), 1.0, 0.0
-        ).astype(BF16)
-        sv = dot(sw[...].reshape(512, 32), rep4)
-        zlane = lax.broadcasted_iota(jnp.int32, (32, 128), 1) // 32
-        for m in modes_of(c):
-            wr = sv[m * 64 : m * 64 + 32]
-            wi = sv[m * 64 + 32 : m * 64 + 64]
-            for r in range(2):
-                for z in range(4):
-                    first = jnp.where(zlane == z, wr if r == 0 else -wi, 0.0)
-                    second = jnp.where(zlane == z, wi if r == 0 else wr, 0.0)
-                    rmat[m, r * 128 + z * 32 : r * 128 + z * 32 + 32, :] = jnp.concatenate([first, second], axis=1).astype(BF16)
-
-    for c in range(2):
-        pl.when(core == c)(functools.partial(mixing_weights, c))
 
     row = lax.broadcasted_iota(jnp.int32, (64, 256), 0)
     col = lax.broadcasted_iota(jnp.int32, (64, 256), 1)
@@ -238,6 +218,29 @@
     for (there, first, _, _), copy in zip(pairs, y_copies):
         pl.when(there & ~first)(copy.start)
 
+    load_s.wait()
+
+    def modes_of(c):
+        return range(SHARE[c][0] // 16, (SHARE[c][0] + SHARE[c][1]) // 16)
+
+    def mixing_weights(c):
+        rep4 = jnp.where(
+            (lax.broadcasted_iota(jnp.int32, (32, 128), 1) & 31) == lax.broadcasted_iota(jnp.int32, (32, 128), 0), 1.0, 0.0
+        ).astype(BF16)
+        sv = dot(sw[...].reshape(512, 32), rep4)
+        zlane = lax.broadcasted_iota(jnp.int32, (32, 128), 1) // 32
+        for m in modes_of(c):
+            wr = sv[m * 64 : m * 64 + 32]
+            wi = sv[m * 64 + 32 : m * 64 + 64]
+            for r in range(2):
+                for z in range(4):
+                    first = jnp.where(zlane == z, wr if r == 0 else -wi, 0.0)
+                    second = jnp.where(zlane == z, wi if r == 0 else wr, 0.0)
+                    rmat[m, r * 128 + z * 32 : r * 128 + z * 32 + 32, :] = jnp.concatenate([first, second], axis=1).astype(BF16)
+
+    for c in range(2):
+        pl.when(core == c)(functools.partial(mixing_weights, c))
+
     lax.fori_loop(FIRST_BANDS, 9, band, 0)
 
     def shift(first, count):
@@ -250,7 +253,6 @@
         shift(1 + b * 32, 32)
         return carry
 
-    lax.fori_loop(0, 4, shift_block, 0)
     for copy in x_copies:
         copy.wait()
     has_left = jnp.where(g > 0, 1.0, 0.0)
@@ -268,6 +270,7 @@
             y_copies[k].start()
             k_copies[k].start()
 
+    lax.fori_loop(0, 4, shift_block, 0)
     greet_later(False)
     fs[1, 0:1] = (xland[0, 1:2].astype(F32) * has_left).astype(BF16)
     fs[1, 129:130] = (xland[1, 0:1].astype(F32) * has_right).astype(BF16)
@@ -333,8 +336,9 @@
     for c in range(2):
         pl.when(core == c)(functools.partial(mix_modes, c))
 
-    lax.fori_loop(2, 4, conv_block, 0, unroll=True)
+    conv_block(2, 0)
     greet_later(True)
+    conv_block(3, 0)
 
     row = lax.broadcasted_iota(jnp.int32, (256, 160), 0)
     col = lax.broadcasted_iota(jnp.int32, (256, 160), 1)

time: 19.2 us -> 18.8 us (0.979)
  the two profiles are of different devices: /device:TPU:227 before, /device:TPU:225 now
where the time goes in v2:
time: 18.8 us; the launch traced here: 18.7 us
  Pallas kernels  17.7 us (94%)
  local copies, waits for them, and re-layouts  0.97 us (5%)
    pallas_call x1, Pallas kernels, shards(): pl.pallas_call(layer_kernel, out_shape=jax.ShapeDtypeStruct(field.shape,...  17.7 us
    unnamed x1, local copies, waits for them, and re-layouts  0.97 us

profile of v2, /device:TPU:225, one launch (start us, length us, event | category | flops | bytes accessed | tf_op | source)
XLA Modules:
  0.0 18.7 jit_solution(14360632410995116746)
XLA Ops:
  0.0 17.7 %layer.1 = bf16[128,8,512]{2,1,0:T(8,128)(2,1)S(1)} custom-call(bf16[128,8,512]{2,1,0:T(8,128)(2,1)} %field.1, bf16[27,32,32]{2,1,0:T(8,128)(2,1)} %convw.1, f32[1,32]{1,0:T(1,128)} %bitcast.1, bf16[32,2,32,32]{3,2,1,0:T(8,128)(2,1)} %specw.1, bf16[8,64,1024]{2,1,0:T(8,128)(2,1)} %constant.4.clone.ftab, bf16[8,1024,512]{2,1,0:T(8,128)(2,1)} %constant.5.clone.itab), custom_call_target="tpu_custom_call" | custom-call | tf_op jit(solution)/shard_map/layer/pallas_call | solution.py:461
  17.7 1.0 %copy.8 = bf16[128,8,512]{2,1,0:T(8,128)(2,1)} copy(bf16[128,8,512]{2,1,0:T(8,128)(2,1)S(1)} %layer.1) | data formatting | bytes 2097152

commit v3 on v2

--- a/solution.py
+++ b/solution.py
@@ -170,17 +170,14 @@
             cbuf[ch, aims(j, 1 - c), :] = part[ch, aims(j, 1 - c), :].astype(BF16)
             c_copy(ch, j, 1 - c).start()
 
-    def answer(k):
-        there, first, dev, lands = pairs[k]
+    for c in range(2):
+        pl.when(core == c)(functools.partial(send_sums, c))
+
+    for there, first, dev, lands in pairs:
 
         @pl.when(there & ~first)
-        def _():
+        def _(dev=dev, lands=lands):
             pl.semaphore_signal(ready.at[lands], inc=1, device_id=dev, device_id_type=MESH)
-
-    answer(1)
-    for c in range(2):
-        pl.when(core == c)(functools.partial(send_sums, c))
-    answer(0)
 
     x_copies = [
         remote(fs.at[1, pl.ds(127, 2)], xland.at[0], x_send.at[0], x_recv.at[0], (right, h)),
@@ -188,17 +185,6 @@
     ]
     for copy in x_copies:
         copy.start()
-    def pass_sums(c):
-        for ch, j in order:
-            c_copy(ch, j, c).wait_recv()
-            if j > 0:
-                total = part[ch, aims(j, c), :] + cland[ch, aims(j, c), :].astype(F32)
-                cbuf[ch, aims(j, c), :] = total.astype(BF16)
-                r_copy(ch, j, c).start()
-
-    for c in range(2):
-        pl.when(core == c)(functools.partial(pass_sums, c))
-
     row = lax.broadcasted_iota(jnp.int32, (64, 256), 0)
     col = lax.broadcasted_iota(jnp.int32, (64, 256), 1)
     pick = jnp.where(col == (row & 31) * 8 + jnp.where(row < 32, 7, 0), 1.0, 0.0).astype(BF16)
@@ -218,6 +204,17 @@
     for (there, first, _, _), copy in zip(pairs, y_copies):
         pl.when(there & ~first)(copy.start)
 
+    def pass_sums(c):
+        for ch, j in order:
+            c_copy(ch, j, c).wait_recv()
+            if j > 0:
+                total = part[ch, aims(j, c), :] + cland[ch, aims(j, c), :].astype(F32)
+                cbuf[ch, aims(j, c), :] = total.astype(BF16)
+                r_copy(ch, j, c).start()
+
+    for c in range(2):
+        pl.when(core == c)(functools.partial(pass_sums, c))
+
     load_s.wait()
 
     def modes_of(c):
@@ -253,6 +250,7 @@
         shift(1 + b * 32, 32)
         return carry
 
+    lax.fori_loop(0, 4, shift_block, 0)
     for copy in x_copies:
         copy.wait()
     has_left = jnp.where(g > 0, 1.0, 0.0)
@@ -270,7 +268,6 @@
             y_copies[k].start()
             k_copies[k].start()
 
-    lax.fori_loop(0, 4, shift_block, 0)
     greet_later(False)
     fs[1, 0:1] = (xland[0, 1:2].astype(F32) * has_left).astype(BF16)
     fs[1, 129:130] = (xland[1, 0:1].astype(F32) * has_right).astype(BF16)
@@ -336,9 +333,9 @@
     for c in range(2):
         pl.when(core == c)(functools.partial(mix_modes, c))
 
-    conv_block(2, 0)
     greet_later(True)
-    conv_block(3, 0)
+
+    lax.fori_loop(2, 4, conv_block, 0, unroll=True)
 
     row = lax.broadcasted_iota(jnp.int32, (256, 160), 0)
     col = lax.broadcasted_iota(jnp.int32, (256, 160), 1)

time: 18.8 us -> 18.2 us (0.968)
  the two profiles are of different devices: /device:TPU:225 before, /device:TPU:1 now
where the time goes in v3:
time: 18.2 us; the launch traced here: 18.1 us
  Pallas kernels  17.1 us (94%)
  local copies, waits for them, and re-layouts  0.97 us (5%)
    pallas_call x1, Pallas kernels, shards(): pl.pallas_call(layer_kernel, out_shape=jax.ShapeDtypeStruct(field.shape,...  17.1 us
    unnamed x1, local copies, waits for them, and re-layouts  0.97 us

profile of v3, /device:TPU:1, one launch (start us, length us, event | category | flops | bytes accessed | tf_op | source)
XLA Modules:
  0.0 18.1 jit_solution(8239702893287430506)
XLA Ops:
  0.0 17.1 %layer.1 = bf16[128,8,512]{2,1,0:T(8,128)(2,1)S(1)} custom-call(bf16[128,8,512]{2,1,0:T(8,128)(2,1)} %field.1, bf16[27,32,32]{2,1,0:T(8,128)(2,1)} %convw.1, f32[1,32]{1,0:T(1,128)} %bitcast.1, bf16[32,2,32,32]{3,2,1,0:T(8,128)(2,1)} %specw.1, bf16[8,64,1024]{2,1,0:T(8,128)(2,1)} %constant.4.clone.ftab, bf16[8,1024,512]{2,1,0:T(8,128)(2,1)} %constant.5.clone.itab), custom_call_target="tpu_custom_call" | custom-call | tf_op jit(solution)/shard_map/layer/pallas_call | solution.py:458
  17.1 1.0 %copy.8 = bf16[128,8,512]{2,1,0:T(8,128)(2,1)} copy(bf16[128,8,512]{2,1,0:T(8,128)(2,1)S(1)} %layer.1) | data formatting | bytes 2097152

commit v4 on v3

--- a/solution.py
+++ b/solution.py
@@ -250,7 +250,6 @@
         shift(1 + b * 32, 32)
         return carry
 
-    lax.fori_loop(0, 4, shift_block, 0)
     for copy in x_copies:
         copy.wait()
     has_left = jnp.where(g > 0, 1.0, 0.0)
@@ -268,6 +267,7 @@
             y_copies[k].start()
             k_copies[k].start()
 
+    lax.fori_loop(0, 4, shift_block, 0)
     greet_later(False)
     fs[1, 0:1] = (xland[0, 1:2].astype(F32) * has_left).astype(BF16)
     fs[1, 129:130] = (xland[1, 0:1].astype(F32) * has_right).astype(BF16)

time: 18.2 us -> 18.5 us (1.016)
  Pallas kernels: 17.1 us -> 17.5 us
    pallas_call x1, Pallas kernels: 17.1 us -> 17.5 us  [shards(): pl.pallas_call(layer_kernel, out_shape=jax.ShapeDtypeStruct(field.shape,...]
where the time goes in v4:
time: 18.5 us; the launch traced here: 18.4 us
  Pallas kernels  17.5 us (95%)
  local copies, waits for them, and re-layouts  0.97 us (5%)
    pallas_call x1, Pallas kernels, shards(): pl.pallas_call(layer_kernel, out_shape=jax.ShapeDtypeStruct(field.shape,...  17.5 us
    unnamed x1, local copies, waits for them, and re-layouts  0.97 us

profile of v4, /device:TPU:1, one launch (start us, length us, event | category | flops | bytes accessed | tf_op | source)
XLA Modules:
  0.0 18.4 jit_solution(2576236212816283287)
XLA Ops:
  0.0 17.5 %layer.1 = bf16[128,8,512]{2,1,0:T(8,128)(2,1)S(1)} custom-call(bf16[128,8,512]{2,1,0:T(8,128)(2,1)} %field.1, bf16[27,32,32]{2,1,0:T(8,128)(2,1)} %convw.1, f32[1,32]{1,0:T(1,128)} %bitcast.1, bf16[32,2,32,32]{3,2,1,0:T(8,128)(2,1)} %specw.1, bf16[8,64,1024]{2,1,0:T(8,128)(2,1)} %constant.4.clone.ftab, bf16[8,1024,512]{2,1,0:T(8,128)(2,1)} %constant.5.clone.itab), custom_call_target="tpu_custom_call" | custom-call | tf_op jit(solution)/shard_map/layer/pallas_call | solution.py:458
  17.5 1.0 %copy.8 = bf16[128,8,512]{2,1,0:T(8,128)(2,1)} copy(bf16[128,8,512]{2,1,0:T(8,128)(2,1)S(1)} %layer.1) | data formatting | bytes 2097152
